TPU v7x, 32 devices: a whole 2x2x4 slice. The times are simulated.
32 devices in a mesh: band: 8 (over z, y), mp: 4 (over x, core).
Axes of the slice: x: 2, y: 2, z: 4, core: 2. Of those that a mesh axis runs over, the one named last changes fastest.
Arguments:
- cells: bfloat16 [2048, 1024], P('band', 'mp'), may hold values from -81 to 81
- row_gain: float32 [1024], replicated, may hold values from 0.1 to 1.9
- row_qkv: bfloat16 [3, 1024, 1024], P(None, None, 'mp'), may hold values from -1.25 to 1.25
- row_out: bfloat16 [1024, 1024], P('mp'), may hold values from -0.1875 to 0.1875
- col_gain: float32 [1024], replicated, may hold values from 0.1 to 1.9
- col_qkv: bfloat16 [3, 1024, 1024], P(None, None, 'mp'), may hold values from -1.25 to 1.25
- col_out: bfloat16 [1024, 1024], P('mp'), may hold values from -0.1875 to 0.1875
- row_seg: int32 [2048], P('band'), may hold values from 0 to 255, never falling along the last dimension, each value on 1 to 16 neighbouring positions
- col_dest: int32 [2048, 1], P('band'), may hold values from 0 to 7; in each aligned block of 256 rows (0 to 255, 256 to 511, ...) at most 48 rows name the same one
- sheet_column_index: int32 [2048], P('band'), may hold values from 1 to 8
- d_result: bfloat16 [2048, 1024], P('band', 'mp'), may hold values from -6 to 6
Outputs:
- result: bfloat16 [2048, 1024], P('band', 'mp')
- d_cells: bfloat16 [2048, 1024], P('band', 'mp')
Inputs may be any that keep to these rules, and one draw needn't show every extreme that they name: `row_seg`: cells never fall in value along the array. `col_dest`: at most 48 of the cells of one row band name the same column band, and some row band sends exactly 48 to some column band.
All inputs are finite; a program needn't handle non-finite values.
Results may differ from a plain program's by a relative error of at most 0.019.
Values may be sent and summed in bfloat16 or wider, within the bound.
A program may use at most 64 MiB of HBM per device.

v0:
```python
import jax
import jax.numpy as jnp
from jax import lax
from jax.sharding import PartitionSpec as P

HEAD_DIM = 64
TILE = 128
norm_eps = 1e-06
neg_fill = -1e30


def block_terms(inputs, norm_gain, query_key_value_weight, w_out, allowed, tile_rows):
    values = inputs.astype(jnp.float32)
    inv_rms = lax.rsqrt(jnp.mean(values * values, axis=-1, keepdims=True) + norm_eps)
    normalized_cells = (values * inv_rms * norm_gain).astype(jnp.bfloat16)
    projected_heads = jnp.einsum(
        "lu,xuh->xlh", normalized_cells, query_key_value_weight, preferred_element_type=jnp.float32
    ).astype(jnp.bfloat16)
    row_count = inputs.shape[0]
    feat_width = query_key_value_weight.shape[2]
    head_count = feat_width // HEAD_DIM
    shaped = projected_heads.reshape(3, row_count // tile_rows, tile_rows, head_count, HEAD_DIM)
    scores = jnp.einsum(
        "bqhe,bkhe->bhqk", shaped[0], shaped[1], preferred_element_type=jnp.float32
    ) * HEAD_DIM ** (-0.5)
    scores = jnp.where(allowed[:, None], scores, neg_fill)
    scores = scores - lax.stop_gradient(jnp.max(scores, axis=-1, keepdims=True))
    expd = jnp.exp(scores)
    attn_probs = (expd / jnp.sum(expd, axis=-1, keepdims=True)).astype(jnp.bfloat16)
    attended = jnp.einsum(
        "bhqk,bkhe->bqhe", attn_probs, shaped[2], preferred_element_type=jnp.float32
    ).astype(jnp.bfloat16)
    attended = attended.reshape(row_count, feat_width)
    return jnp.dot(attended, w_out, preferred_element_type=jnp.float32)


def column_band_mask(col_keys):
    positions = jnp.arange(col_keys.shape[0])
    same_col = (col_keys[:, None] == col_keys[None, :]) & (col_keys[None, :] > 0)
    return (same_col | (positions[:, None] == positions[None, :]))[None]


def widen(block):
    return lax.all_gather(block, "mp", axis=1, tiled=True)


def narrow(terms):
    return lax.psum_scatter(
        terms.astype(jnp.bfloat16), "mp", scatter_dimension=1, tiled=True
    ).astype(jnp.float32)


def move_rows(rows):
    return lax.all_to_all(rows, "band", split_axis=0, concat_axis=0, tiled=True)


def on_device(
    cells,
    row_gain,
    row_qkv,
    row_out,
    col_gain,
    col_qkv,
    col_out,
    row_seg,
    col_dest,
    sheet_column_index,
    d_result,
):
    cell_rows, feat_width = cells.shape
    band_count = lax.axis_size("band")
    capacity = max(2, 3 * cell_rows // (2 * band_count))
    slot_total = band_count * capacity
    gathered = widen(cells)
    row_groups = row_seg.reshape(cell_rows // TILE, TILE)
    row_mask = row_groups[:, :, None] == row_groups[:, None, :]

    def row_local(inputs):
        return block_terms(inputs, row_gain, row_qkv, row_out, row_mask, TILE)

    row_terms, row_pull = jax.vjp(row_local, gathered)
    target = col_dest[:, 0]
    onehot = (target[:, None] == jnp.arange(band_count, dtype=jnp.int32)[None, :]).astype(jnp.int32)
    ranking = jnp.sum((jnp.cumsum(onehot, axis=0) - onehot) * onehot, axis=1)
    slot_index = target * capacity + ranking
    keys_out = (
        jnp.zeros((slot_total,), jnp.bfloat16)
        .at[slot_index]
        .set(sheet_column_index.astype(jnp.bfloat16))
    )
    back_in = jnp.zeros((slot_total, feat_width), jnp.bfloat16).at[slot_index].set(d_result)
    mixed_rows = (cells.astype(jnp.float32) + narrow(row_terms)).astype(jnp.bfloat16)
    outgoing = jnp.zeros((slot_total, feat_width), jnp.bfloat16).at[slot_index].set(mixed_rows)
    arrived, col_keys = (
        lax.all_to_all(outgoing, "band", split_axis=0, concat_axis=0, tiled=True),
        lax.all_to_all(keys_out, "band", split_axis=0, concat_axis=0, tiled=True),
    )
    column_full = widen(arrived)
    col_allowed = column_band_mask(col_keys)

    def col_local(inputs):
        return block_terms(inputs, col_gain, col_qkv, col_out, col_allowed, inputs.shape[0])

    col_terms, col_pull = jax.vjp(col_local, column_full)
    settled = (arrived.astype(jnp.float32) + narrow(col_terms)).astype(jnp.bfloat16)
    result = move_rows(settled)[slot_index]
    d_column = move_rows(back_in)
    (d_col_part,) = col_pull(widen(d_column).astype(jnp.float32))
    d_mixed_col = (d_column.astype(jnp.float32) + narrow(d_col_part.astype(jnp.float32))).astype(
        jnp.bfloat16
    )
    d_mixed = move_rows(d_mixed_col)[slot_index]
    (d_row_part,) = row_pull(widen(d_mixed).astype(jnp.float32))
    d_cells = (d_mixed.astype(jnp.float32) + narrow(d_row_part.astype(jnp.float32))).astype(
        jnp.bfloat16
    )
    return (result, d_cells)


def solution(mesh):
    in_specs = (
        P("band", "mp"),
        P(),
        P(None, None, "mp"),
        P("mp", None),
        P(),
        P(None, None, "mp"),
        P("mp", None),
        P("band"),
        P("band", None),
        P("band"),
        P("band", "mp"),
    )
    out_specs = (P("band", "mp"), P("band", "mp"))
    return jax.shard_map(
        on_device, mesh=mesh, in_specs=in_specs, out_specs=out_specs, check_vma=False
    )
```

profile of v0, /device:TPU:0, one launch (start us, length us, event | category | flops | bytes accessed | tf_op | source)
XLA Modules:
  0.0 187.3 jit_solution(5068009255196758206)
XLA Ops:
  7.2 9.0 %all_gather.12 = bf16[256,1024]{1,0:T(8,128)(2,1)S(1)} all-gather(bf16[256,256]{1,0:T(8,128)(2,1)} %param.11), channel_id=1, replica_groups=mesh['band'=8,'mp'=4] {'mp'}, dimensions={1}, use_global_device_ids=true | all-gather | bytes 655360 | tf_op jit(solution)/shard_map/all_gather | solution.py:44
  16.2 0.2 fusion.34
  16.4 2.1 %fusion.21 = bf16[3,256,256]{2,1,0:T(8,128)(2,1)S(1)} fusion(bf16[3,1024,256]{2,1,0:T(8,128)(2,1)} %param.13, bf16[256,1024]{1,0:T(8,128)(2,1)S(1)} %all_gather.12, f32[1024]{0:T(1024)} %param.12, f32[256]{0:T(256)S(1)} %fusion.63), kind=kOutput, calls=%fused_computation.50 | convolution fusion | flops 403898368 | bytes 2495488 | tf_op jit(solution)/shard_map/jvp(lu,xuh->xlh)/dot_general | solution.py:16
  18.5 0.2 reshape.325
  18.7 0.2 copy.58
  18.8 0.2 reshape.326
  19.0 0.2 copy.59
  19.3 0.2 reshape.324
  19.5 0.2 copy.60
  19.7 1.2 fusion.75
  20.9 1.3 fusion.29
  22.2 0.1 copy.62
  22.3 1.1 convolution_convert_fusion.3
  23.5 0.6 reduce-window.6
  24.1 0.2 slice_reduce_fusion
  24.4 2.2 %scatter_custom_fusion.1 = bf16[384]{0:T(512)(128)(2,1)S(1)} fusion(s32[256]{0:T(256)S(1)} %bitcast.165, bf16[256]{0:T(256)(128)(2,1)S(1)} %convert_element_type.209, bf16[]{:T(256)} %constant.12.clone.1), kind=kCustom, calls=%fused_computation.125 | custom fusion | bytes 770 | tf_op jit(solution)/shard_map/scatter | solution.py:89
  26.6 0.7 all_to_all.52
  27.3 5.8 %all-to-all-start.1 = ((bf16[8,48,1]{1,2,0:T(2,128)(2,1)}), bf16[8,48,1]{1,2,0:T(2,128)(2,1)S(1)}, u32[]{:S(2)}, u32[]{:S(2)}) async-start(bf16[8,48,1]{1,2,0:T(2,128)(2,1)} %all_to_all.52), calls=%async_computation.2 | async-start | bytes 8192 | tf_op jit(solution)/shard_map/all_to_all | solution.py:96
  33.1 2.5 %scatter_custom_fusion.2 = bf16[384,256]{1,0:T(8,128)(2,1)} fusion(s32[256]{0:T(256)S(1)} %bitcast.166, bf16[256,256]{1,0:T(8,128)(2,1)} %param.21, bf16[]{:T(256)} %constant.12.clone.1), kind=kCustom, calls=%fused_computation.103 | custom fusion | bytes 197120 | tf_op jit(solution)/shard_map/scatter | solution.py:91
  35.6 4.0 %all-to-all-done.1 = bf16[8,48,1]{1,2,0:T(2,128)(2,1)S(1)} async-done(((bf16[8,48,1]{1,2,0:T(2,128)(2,1)}), bf16[8,48,1]{1,2,0:T(2,128)(2,1)S(1)}, u32[]{:S(2)}, u32[]{:S(2)}) %all-to-all-start.1) | async-done | bytes 800 | tf_op jit(solution)/shard_map/all_to_all | solution.py:96
  39.6 3.4 %all-to-all-start.3 = ((bf16[8,48,256]{2,1,0:T(8,128)(2,1)}), bf16[8,48,256]{2,1,0:T(8,128)(2,1)S(1)}, u32[]{:S(2)}, u32[]{:S(2)}) async-start(bf16[8,48,256]{2,1,0:T(8,128)(2,1)} %bitcast.22), calls=%async_computation.5 | async-start | bytes 393216 | tf_op jit(solution)/shard_map/all_to_all | solution.py:54
  43.1 0.8 fusion.43
  43.9 2.2 %reduce-scatter.5.cloned.1.call-done = bf16[256,256]{1,0:T(8,128)(2,1)} async-done(((bf16[256,1024]{1,0:T(8,128)(2,1)}), bf16[256,256]{1,0:T(8,128)(2,1)}) %reduce-scatter.5.cloned.1.call-update) | async-done | bytes 131088 | tf_op jit(solution)/shard_map/reduce_scatter | solution.py:48
  46.2 2.5 %scatter_custom_fusion = bf16[384,256]{1,0:T(8,128)(2,1)} fusion(s32[256]{0:T(256)S(1)} %bitcast.167, bf16[256,256]{1,0:T(8,128)(2,1)} %reduce-scatter.5.cloned.1.call-done, bf16[256,256]{1,0:T(8,128)(2,1)S(1)} %copy-done.12, bf16[]{:T(256)} %constant.12.clone.1), kind=kCustom, calls=%fused_computation.98 | custom fusion | flops 262144 | bytes 458754 | tf_op jit(solution)/shard_map/scatter | solution.py:93
  48.6 2.1 %all-to-all-done.3 = bf16[8,48,256]{2,1,0:T(8,128)(2,1)S(1)} async-done(((bf16[8,48,256]{2,1,0:T(8,128)(2,1)}), bf16[8,48,256]{2,1,0:T(8,128)(2,1)S(1)}, u32[]{:S(2)}, u32[]{:S(2)}) %all-to-all-start.3) | async-done | bytes 196640 | tf_op jit(solution)/shard_map/all_to_all | solution.py:54
  50.7 3.6 %all-to-all-start = ((bf16[8,48,256]{2,1,0:T(8,128)(2,1)}), bf16[8,48,256]{2,1,0:T(8,128)(2,1)S(1)}, u32[]{:S(2)}, u32[]{:S(2)}) async-start(bf16[8,48,256]{2,1,0:T(8,128)(2,1)} %bitcast.10), calls=%async_computation.1 | async-start | bytes 393216 | tf_op jit(solution)/shard_map/all_to_all | solution.py:95
  54.3 8.0 %all_gather.14 = bf16[384,1024]{1,0:T(8,128)(2,1)S(1)} all-gather(bf16[384,256]{1,0:T(8,128)(2,1)S(1)} %bitcast.146), channel_id=1, replica_groups=mesh['band'=8,'mp'=4] {'mp'}, dimensions={1}, use_global_device_ids=true | all-gather | bytes 983040 | tf_op jit(solution)/shard_map/all_gather | solution.py:44
  62.4 0.5 convolution_convert_fusion.9
  62.9 8.9 %all_gather.13 = bf16[384,1024]{1,0:T(8,128)(2,1)S(1)} all-gather(bf16[384,256]{1,0:T(8,128)(2,1)S(1)} %bitcast.145), channel_id=1, replica_groups=mesh['band'=8,'mp'=4] {'mp'}, dimensions={1}, use_global_device_ids=true | all-gather | bytes 983040 | tf_op jit(solution)/shard_map/all_gather | solution.py:44
  71.8 0.2 fusion.10
  72.0 1.1 fusion.18
  73.1 0.8 fusion.73
  74.0 3.5 %fusion.76 = (f32[4,384]{1,0:T(4,128)S(1)}, f32[4,384,384]{1,2,0:T(8,128)}) fusion(pred[384,384]{0,1:T(8,128)(4,1)} %fusion.43, bf16[384,4,64]{0,2,1:T(8,128)(2,1)} %bitcast.159, bf16[384,4,64]{0,2,1:T(8,128)(2,1)} %bitcast.156), kind=kOutput, calls=%fused_computation.135 | convolution fusion | flops 77857152 | bytes 2906112 | tf_op jit(solution)/shard_map/jvp()/sub | solution.py:27
  77.5 3.7 %fusion.7 = (f32[4,384]{1,0:T(4,128)S(1)}, bf16[4,384,384]{1,2,0:T(8,128)(2,1)}, bf16[4,384,384]{1,2,0:T(8,128)(2,1)}) fusion(f32[4,384,384]{1,2,0:T(8,128)} %get-tuple-element.13, f32[4,384]{1,0:T(4,128)S(1)} %multiply_divide_fusion, f32[4,384]{1,0:T(4,128)S(1)} %get-tuple-element.12, bf16[4,64,384]{2,1,0:T(8,128)(2,1)S(1)} %bitcast.150, ...), kind=kOutput, calls=%fused_computation.19 | convolution fusion | flops 79624704 | bytes 5130240 | tf_op jit(solution)/shard_map/transpose(jvp(bhqk,bkhe->bqhe))/dot_general | solution.py:30
  81.2 3.9 %fusion.26 = bf16[1,1,384,4,64]{2,4,3,1,0:T(8,128)(2,1)} fusion(bf16[384,4,64]{0,2,1:T(8,128)(2,1)} %bitcast.160, bf16[4,384,384]{1,2,0:T(8,128)(2,1)} %get-tuple-element.14, f32[4,384]{1,0:T(4,128)S(1)} %neg.13, f32[4,384]{1,0:T(4,128)S(1)} %get-tuple-element.12, pred[384,384]{0,1:T(8,128)(4,1)} %fusion.43, bf16[384,4,64]{0,2,1:T(8,128)(2,1)S(1)} %bitcast.157), kind=kOutput, calls=%fused_computation.61 | convolution fusion | flops 156403584 | bytes 1929216 | tf_op jit(solution)/shard_map/transpose(jvp(bqhe,bkhe->bhqk))/dot_general | solution.py:23
  85.2 3.6 %fusion.27 = bf16[1,1,384,4,64]{2,4,3,1,0:T(8,128)(2,1)} fusion(bf16[384,4,64]{0,2,1:T(8,128)(2,1)S(1)} %bitcast.158, bf16[4,384,384]{1,2,0:T(8,128)(2,1)} %get-tuple-element.14, f32[4,384]{1,0:T(4,128)S(1)} %neg.13, f32[4,384]{1,0:T(4,128)S(1)} %get-tuple-element.12, pred[384,384]{0,1:T(8,128)(4,1)} %fusion.43, bf16[384,4,64]{0,2,1:T(8,128)(2,1)S(1)} %bitcast.161), kind=kOutput, calls=%fused_computation.62 | convolution fusion | flops 156403584 | bytes 1929216 | tf_op jit(solution)/shard_map/transpose(jvp(bqhe,bkhe->bhqk))/dot_general | solution.py:23
  88.8 1.8 fusion.28
  90.6 1.1 pad_add_fusion
  91.7 1.1 copy.69
  92.8 2.0 %fusion.13 = (f32[384]{0:T(512)S(1)}, bf16[384,1024]{1,0:T(8,128)(2,1)S(1)}) fusion(bf16[384,1024]{1,0:T(8,128)(2,1)S(1)} %all_gather.13, f32[1024]{0:T(1024)S(1)} %copy-done.20, bf16[3,1024,256]{2,1,0:T(8,128)(2,1)S(1)} %copy-done, bf16[3,384,256]{2,1,0:T(8,128)(2,1)} %copy.69), kind=kOutput, calls=%fused_computation.32 | convolution fusion | flops 606338688 | bytes 3741184 | tf_op jit(solution)/shard_map/transpose(jvp(lu,xuh->xlh))/dot_general | solution.py:16
  94.8 1.3 fusion.9
  96.1 24.4 %reduce-scatter.9.cloned.1.call-done = bf16[384,256]{1,0:T(8,128)(2,1)} async-done(((bf16[384,1024]{1,0:T(8,128)(2,1)}), bf16[384,256]{1,0:T(8,128)(2,1)}) %reduce-scatter.9.cloned.1.call-update) | async-done | bytes 196624 | tf_op jit(solution)/shard_map/reduce_scatter | solution.py:48
  120.5 1.7 add_convert_fusion
  122.3 5.5 %all-to-all-start.4 = ((bf16[8,48,256]{2,1,0:T(8,128)(2,1)}), bf16[8,48,256]{2,1,0:T(8,128)(2,1)S(1)}, u32[]{:S(2)}, u32[]{:S(2)}) async-start(bf16[8,48,256]{2,1,0:T(8,128)(2,1)} %bitcast.41), calls=%async_computation.7 | async-start | bytes 393216 | tf_op jit(solution)/shard_map/all_to_all | solution.py:54
  127.8 1.7 convolution_convert_fusion.10
  129.6 1.3 convolution_convert_fusion.1
  130.9 4.8 %all-to-all-done.4 = bf16[8,48,256]{2,1,0:T(8,128)(2,1)S(1)} async-done(((bf16[8,48,256]{2,1,0:T(8,128)(2,1)}), bf16[8,48,256]{2,1,0:T(8,128)(2,1)S(1)}, u32[]{:S(2)}, u32[]{:S(2)}) %all-to-all-start.4) | async-done | bytes 196640 | tf_op jit(solution)/shard_map/all_to_all | solution.py:54
  135.8 1.2 gather_fusion.1
  136.9 6.7 %all-gather = bf16[256,1024]{1,0:T(8,128)(2,1)S(1)} all-gather(bf16[256,256]{1,0:T(8,128)(2,1)S(1)} %gather_fusion.1), channel_id=2, replica_groups=mesh['band'=8,'mp'=4] {'mp'}, dimensions={1}, use_global_device_ids=true | all-gather | bytes 655360 | tf_op jit(solution)/shard_map/all_gather | solution.py:44
  143.6 0.3 convolution_convert_fusion.14
  144.2 1.3 multiply_reduce_fusion
  145.5 1.4 fusion.30
  146.9 0.2 fusion.32
  147.2 0.3 fusion.31
  147.5 0.4 copy.79
  147.9 0.3 reshape.278
  148.2 2.2 %fusion.37 = (f32[256]{0:T(256)S(1)}, f32[256,1024]{1,0:T(8,128)S(1)}) fusion(bf16[256,1024]{1,0:T(8,128)(2,1)S(1)} %all_gather.12, f32[1024]{0:T(1024)S(1)} %copy-done.21, bf16[3,1024,256]{2,1,0:T(8,128)(2,1)} %param.13, bf16[3,256,256]{1,2,0:T(8,128)(2,1)S(1)} %reshape.278), kind=kOutput, calls=%fused_computation.77 | convolution fusion | flops 404225792 | bytes 3544064 | tf_op jit(solution)/shard_map/transpose(jvp(lu,xuh->xlh))/dot_general | solution.py:16
  150.4 1.1 fusion.33
  151.5 3.5 %reduce-scatter.7.cloned.1.call-done = bf16[384,256]{1,0:T(8,128)(2,1)} async-done(((bf16[384,1024]{1,0:T(8,128)(2,1)}), bf16[384,256]{1,0:T(8,128)(2,1)}) %reduce-scatter.7.cloned.1.call-update) | async-done | bytes 196624 | tf_op jit(solution)/shard_map/reduce_scatter | solution.py:48
  155.0 1.0 add_convert_fusion.1
  155.9 13.3 %all_to_all.58 = bf16[8,48,256]{2,1,0:T(8,128)(2,1)S(1)} all-to-all(bf16[8,48,256]{2,1,0:T(8,128)(2,1)S(1)} %bitcast.149), channel_id=1, replica_groups=mesh['band'=8,'mp'=4] {'band'}, dimensions={0} | all-to-all | bytes 393216 | tf_op jit(solution)/shard_map/all_to_all | solution.py:54
  169.2 1.8 gather_fusion
  171.0 8.2 %reduce-scatter.11.cloned.1.call-done = bf16[256,256]{1,0:T(8,128)(2,1)} async-done(((bf16[256,1024]{1,0:T(8,128)(2,1)}), bf16[256,256]{1,0:T(8,128)(2,1)}) %reduce-scatter.11.cloned.1.call-update) | async-done | bytes 131088 | tf_op jit(solution)/shard_map/reduce_scatter | solution.py:48
  179.2 1.6 add_convert_fusion.2
  (80 shorter events, 1.0 us)
Async XLA Ops:
  7.2 64.8 %copy-start = (bf16[3,1024,256]{2,1,0:T(8,128)(2,1)S(1)}, bf16[3,1024,256]{2,1,0:T(8,128)(2,1)}, u32[]{:S(2)}) copy-start(bf16[3,1024,256]{2,1,0:T(8,128)(2,1)} %param.16) | copy-start | bytes 4718596
  7.2 39.0 %reduce-scatter.5.cloned.1.call-start = ((), (), s32[]{:S(2)}) async-start(), calls=%async_computation.9 | async-start | bytes 655360 | tf_op jit(solution)/shard_map/reduce_scatter | solution.py:48
  16.4 2.8 %copy-start.22 = (s32[256]{0:T(256)S(1)}, s32[256]{0:T(256)}, u32[]{:S(2)}) copy-start(s32[256]{0:T(256)} %param.18) | copy-start | bytes 3076
  18.8 2.0 %copy-start.15 = (bf16[2,128,4,64]{1,3,2,0:T(8,128)(2,1)}, bf16[2,128,4,64]{1,3,2,0:T(8,128)(2,1)S(1)}, u32[]{:S(2)}) copy-start(bf16[2,128,4,64]{1,3,2,0:T(8,128)(2,1)S(1)} %copy.58) | copy-start | bytes 393220
  19.0 3.3 %copy-start.3 = (bf16[256,1024]{1,0:T(8,128)(2,1)S(1)}, bf16[256,1024]{1,0:T(8,128)(2,1)}, u32[]{:S(2)}) copy-start(bf16[256,1024]{1,0:T(8,128)(2,1)} %param.14) | copy-start | bytes 1572868
  19.2 1.7 copy-start.17
  19.6 1.2 copy-start.9
  19.6 3.8 %copy-start.19 = (s32[256,1]{0,1:T(1,128)S(1)}, s32[256,1]{0,1:T(1,128)}, u32[]{:S(2)}) copy-start(s32[256,1]{0,1:T(1,128)} %param.19) | copy-start | bytes 3076
  19.6 4.7 %copy-start.23 = (s32[256]{0:T(256)S(1)}, s32[256]{0:T(256)}, u32[]{:S(2)}) copy-start(s32[256]{0:T(256)} %param.20) | copy-start | bytes 3076
  20.9 25.3 %copy-start.12 = (bf16[256,256]{1,0:T(8,128)(2,1)S(1)}, bf16[256,256]{1,0:T(8,128)(2,1)}, u32[]{:S(2)}) copy-start(bf16[256,256]{1,0:T(8,128)(2,1)} %param.11) | copy-start | bytes 393220
  22.2 40.2 %copy-start.1 = (bf16[256,1024]{1,0:T(8,128)(2,1)S(1)}, bf16[256,1024]{1,0:T(8,128)(2,1)}, u32[]{:S(2)}) copy-start(bf16[256,1024]{1,0:T(8,128)(2,1)} %param.17) | copy-start | bytes 1572868
  27.3 12.3 %all-to-all-start.1 = ((bf16[8,48,1]{1,2,0:T(2,128)(2,1)}), bf16[8,48,1]{1,2,0:T(2,128)(2,1)S(1)}, u32[]{:S(2)}, u32[]{:S(2)}) async-start(bf16[8,48,1]{1,2,0:T(2,128)(2,1)} %all_to_all.52), calls=%async_computation.2 | async-start | bytes 8192 | tf_op jit(solution)/shard_map/all_to_all | solution.py:96
  39.6 11.1 %all-to-all-start.3 = ((bf16[8,48,256]{2,1,0:T(8,128)(2,1)}), bf16[8,48,256]{2,1,0:T(8,128)(2,1)S(1)}, u32[]{:S(2)}, u32[]{:S(2)}) async-start(bf16[8,48,256]{2,1,0:T(8,128)(2,1)} %bitcast.22), calls=%async_computation.5 | async-start | bytes 393216 | tf_op jit(solution)/shard_map/all_to_all | solution.py:54
  48.6 23.4 %copy-start.20 = (f32[1024]{0:T(1024)S(1)}, f32[1024]{0:T(1024)}, u32[]{:S(2)}) copy-start(f32[1024]{0:T(1024)} %param.15) | copy-start | bytes 12292
  50.7 12.1 %copy-start.7 = (bf16[8,48,256]{2,1,0:T(8,128)(2,1)}, bf16[8,48,256]{2,1,0:T(8,128)(2,1)S(1)}, u32[]{:S(2)}) copy-start(bf16[8,48,256]{2,1,0:T(8,128)(2,1)S(1)} %all-to-all-done.3) | copy-start | bytes 589828
  50.7 12.1 %all-to-all-start = ((bf16[8,48,256]{2,1,0:T(8,128)(2,1)}), bf16[8,48,256]{2,1,0:T(8,128)(2,1)S(1)}, u32[]{:S(2)}, u32[]{:S(2)}) async-start(bf16[8,48,256]{2,1,0:T(8,128)(2,1)} %bitcast.10), calls=%async_computation.1 | async-start | bytes 393216 | tf_op jit(solution)/shard_map/all_to_all | solution.py:95
  54.3 66.2 %reduce-scatter.9.cloned.1.call-start = ((), (), s32[]{:S(2)}) async-start(), calls=%async_computation.11 | async-start | bytes 983040 | tf_op jit(solution)/shard_map/reduce_scatter | solution.py:48
  62.8 10.3 %copy-start.5 = (bf16[8,48,256]{2,1,0:T(8,128)(2,1)}, bf16[8,48,256]{2,1,0:T(8,128)(2,1)S(1)}, u32[]{:S(2)}) copy-start(bf16[8,48,256]{2,1,0:T(8,128)(2,1)S(1)} %all-to-all-done) | copy-start | bytes 589828
  73.9 7.3 %copy-start.8 = (bf16[1,384,256]{1,2,0:T(8,128)(2,1)}, bf16[1,384,256]{1,2,0:T(8,128)(2,1)S(1)}, u32[]{:S(2)}) copy-start(bf16[1,384,256]{1,2,0:T(8,128)(2,1)S(1)} %get-tuple-element.6) | copy-start | bytes 589828
  77.5 3.7 %copy-start.13 = (bf16[1,384,256]{1,2,0:T(8,128)(2,1)S(1)}, bf16[1,384,256]{1,2,0:T(8,128)(2,1)}, u32[]{:S(2)}) copy-start(bf16[1,384,256]{1,2,0:T(8,128)(2,1)} %get-tuple-element.4) | copy-start | bytes 589828
  81.2 3.9 %copy-start.14 = (bf16[1,384,256]{1,2,0:T(8,128)(2,1)S(1)}, bf16[1,384,256]{1,2,0:T(8,128)(2,1)}, u32[]{:S(2)}) copy-start(bf16[1,384,256]{1,2,0:T(8,128)(2,1)} %get-tuple-element.5) | copy-start | bytes 589828
  94.8 34.8 %copy-start.2 = (bf16[256,1024]{1,0:T(8,128)(2,1)S(1)}, bf16[256,1024]{1,0:T(8,128)(2,1)}, u32[]{:S(2)}) copy-start(bf16[256,1024]{1,0:T(8,128)(2,1)} %param.17) | copy-start | bytes 1572868
  122.3 13.5 %all-to-all-start.4 = ((bf16[8,48,256]{2,1,0:T(8,128)(2,1)}), bf16[8,48,256]{2,1,0:T(8,128)(2,1)S(1)}, u32[]{:S(2)}, u32[]{:S(2)}) async-start(bf16[8,48,256]{2,1,0:T(8,128)(2,1)} %bitcast.41), calls=%async_computation.7 | async-start | bytes 393216 | tf_op jit(solution)/shard_map/all_to_all | solution.py:54
  127.8 27.2 %reduce-scatter.7.cloned.1.call-start = ((), (), s32[]{:S(2)}) async-start(), calls=%async_computation.10 | async-start | bytes 983040 | tf_op jit(solution)/shard_map/reduce_scatter | solution.py:48
  129.5 14.1 %copy-start.4 = (bf16[256,1024]{1,0:T(8,128)(2,1)S(1)}, bf16[256,1024]{1,0:T(8,128)(2,1)}, u32[]{:S(2)}) copy-start(bf16[256,1024]{1,0:T(8,128)(2,1)} %param.14) | copy-start | bytes 1572868
  130.8 13.3 %copy-start.10 = (bf16[2,128,4,64]{1,3,2,0:T(8,128)(2,1)S(1)}, bf16[2,128,4,64]{1,3,2,0:T(8,128)(2,1)}, u32[]{:S(2)}) copy-start(bf16[2,128,4,64]{1,3,2,0:T(8,128)(2,1)} %copy-done.9) | copy-start | bytes 393220
  130.9 48.3 %reduce-scatter.11.cloned.1.call-start = ((), (), s32[]{:S(2)}) async-start(), calls=%async_computation.12 | async-start | bytes 655360 | tf_op jit(solution)/shard_map/reduce_scatter | solution.py:48
  143.6 3.2 %copy-start.18 = (bf16[2,128,4,64]{1,3,2,0:T(8,128)(2,1)S(1)}, bf16[2,128,4,64]{1,3,2,0:T(8,128)(2,1)}, u32[]{:S(2)}) copy-start(bf16[2,128,4,64]{1,3,2,0:T(8,128)(2,1)} %copy-done.17) | copy-start | bytes 393220
  144.0 2.9 %copy-start.11 = (f32[2,4,128,128]{2,3,1,0:T(8,128)S(1)}, f32[2,4,128,128]{2,3,1,0:T(8,128)}, u32[]{:S(2)}) copy-start(f32[2,4,128,128]{2,3,1,0:T(8,128)} %get-tuple-element.11) | copy-start | bytes 1572868
  145.5 1.7 copy-start.16
  147.2 1.0 copy-start.21
  148.2 6.7 %copy-start.6 = (bf16[8,48,256]{2,1,0:T(8,128)(2,1)S(1)}, bf16[8,48,256]{2,1,0:T(8,128)(2,1)}, u32[]{:S(2)}) copy-start(bf16[8,48,256]{2,1,0:T(8,128)(2,1)} %copy-done.5) | copy-start | bytes 589828
Sparse Core Ops, SparseCore 0:
  23.6 22.5 reduce-scatter.4
  96.2 24.2 reduce-scatter.8
  131.2 23.7 reduce-scatter.6
  157.4 21.6 reduce-scatter.10
where the time goes:
time: 188 us; the launch traced here: 187 us
  waiting for transfers between devices  49.2 us (26%)
  blocking collectives  45.9 us (24%)
  matrix products  34.5 us (18%)
  starting transfers between devices  18.5 us (10%)
  between operations  14.3 us (8%)
  local copies, waits for them, and re-layouts  12.5 us (7%)
  other arithmetic  12.5 us (7%)
    reduce_scatter x4, waiting for transfers between devices, narrow(): lax.psum_scatter(terms.astype(jnp.bfloat16), 'mp', scatter_dimension=1, t...  38.2 us
    all_gather x4, blocking collectives, widen(): return lax.all_gather(block, 'mp', axis=1, tiled=True)  32.6 us
    all_to_all x1, blocking collectives, move_rows(): return lax.all_to_all(rows, 'band', split_axis=0, concat_axis=0, tiled=True)  13.3 us
    dot_general x6, matrix products, block_terms(): jnp.einsum('bhqk,bkhe->bqhe', attn_probs, shaped[2], preferred_element_ty...  11.2 us
    all_to_all x2, starting transfers between devices, move_rows(): return lax.all_to_all(rows, 'band', split_axis=0, concat_axis=0, tiled=True)  8.9 us
    dot_general x4, matrix products, block_terms(): jnp.einsum('bqhe,bkhe->bhqk', shaped[0], shaped[1], preferred_element_typ...  8.12 us
    dot_general x4, matrix products, block_terms(): jnp.einsum('lu,xuh->xlh', normalized_cells, query_key_value_weight, prefe...  7.28 us
    all_to_all x2, waiting for transfers between devices, move_rows(): return lax.all_to_all(rows, 'band', split_axis=0, concat_axis=0, tiled=True)  6.91 us
  transfers between devices with their start and end apart: 8, of which 7 were waited for; matrix products, arithmetic and copies ran while one was open for 13% of the time, Pallas kernels for 0%

commit v1 on v0

--- a/solution.py
+++ b/solution.py
@@ -1,3 +1,4 @@
+import functools
 import jax
 import jax.numpy as jnp
 from jax import lax
@@ -7,6 +8,27 @@
 TILE = 128
 norm_eps = 1e-06
 neg_fill = -1e30
+
+
+def link_boxes(m, ndim_at):
+    z_new = list(m.shape[1:])
+    z_new[ndim_at] *= m.shape[0]
+    return jnp.moveaxis(m, 0, ndim_at).reshape(z_new)
+
+
+def expand_frame_on(view, comm_axis, row_dim):
+    size_here = jax.lax.axis_size(comm_axis)
+    in_order = [(pp, (pp + 1) % size_here) for pp in range(size_here)]
+    cards = [view]
+    while len(cards) < size_here:
+        cards.append(jax.lax.ppermute(cards[-1], comm_axis, in_order))
+    then = jax.lax.axis_index(comm_axis)
+    e_now = jnp.stack(cards)
+    cards = e_now[(then - jnp.arange(size_here)) % size_here]
+    return link_boxes(cards, row_dim)
+
+
+work_series_all = functools.partial(expand_frame_on, comm_axis="mp", row_dim=1)
 
 
 def block_terms(inputs, norm_gain, query_key_value_weight, w_out, allowed, tile_rows):
@@ -41,7 +63,7 @@
 
 
 def widen(block):
-    return lax.all_gather(block, "mp", axis=1, tiled=True)
+    return work_series_all(block)
 
 
 def narrow(terms):

time: 188 us -> 238 us (1.27)
  waiting for transfers between devices: 49.2 us -> 91 us
  blocking collectives: 45.9 us -> 13.3 us
  local copies, waits for them, and re-layouts: 12.5 us -> 35.6 us
  other arithmetic: 12.5 us -> 24.1 us
  matrix products: 34.5 us -> 37.1 us
    ppermute x0 -> x12, waiting for transfers between devices: none -> 36.9 us  [expand_frame_on(): cards.append(jax.lax.ppermute(cards[-1], comm_axis, in_order))]
    all_gather x4 -> x0, blocking collectives: 32.6 us -> none  [widen(): return lax.all_gather(block, 'mp', axis=1, tiled=True)]
    gather x0 -> x4, local copies, waits for them, and re-layouts: none -> 6.63 us  [expand_frame_on(): cards = e_now[(then - jnp.arange(size_here)) % size_here]]
    another operation x2 -> x6, other arithmetic: 0.62 us -> 6.96 us  [the longest x4 6.33 us: expand_frame_on(): e_now = jnp.stack(cards)]
    convert_element_type x0 -> x3, local copies, waits for them, and re-layouts: none -> 6.2 us  [block_terms(): values = inputs.astype(jnp.float32)]
    transpose x0 -> x2, local copies, waits for them, and re-layouts: none -> 3.54 us  [link_boxes(): return jnp.moveaxis(m, 0, ndim_at).reshape(z_new)]
    unnamed x48 -> x84, local copies, waits for them, and re-layouts: 0.13 us -> 2.93 us
    dot_general x4, matrix products: 3.18 us -> 5.95 us  [block_terms(): return jnp.dot(attended, w_out, preferred_element_type=jnp.float32)]
  transfers between devices with their start and end apart: 8 -> 20, of which waited for: 7 -> 19; matrix products, arithmetic and copies ran while one was open for 13% -> 17% of each run, Pallas kernels for 0% -> 0%
where the time goes in v1:
time: 238 us; the launch traced here: 236 us
  waiting for transfers between devices  91 us (38%)
  matrix products  37.1 us (16%)
  local copies, waits for them, and re-layouts  35.6 us (15%)
  other arithmetic  24.1 us (10%)
  starting transfers between devices  20.7 us (9%)
  between operations  14.5 us (6%)
  blocking collectives  13.3 us (6%)
    reduce_scatter x4, waiting for transfers between devices, narrow(): lax.psum_scatter(terms.astype(jnp.bfloat16), 'mp', scatter_dimension=1, t...  37.7 us
    ppermute x12, waiting for transfers between devices, expand_frame_on(): cards.append(jax.lax.ppermute(cards[-1], comm_axis, in_order))  36.9 us
    all_to_all x1, blocking collectives, move_rows(): return lax.all_to_all(rows, 'band', split_axis=0, concat_axis=0, tiled=True)  13.3 us
    dot_general x6, matrix products, block_terms(): jnp.einsum('bhqk,bkhe->bqhe', attn_probs, shaped[2], preferred_element_ty...  11.2 us
    all_to_all x2, waiting for transfers between devices, move_rows(): return lax.all_to_all(rows, 'band', split_axis=0, concat_axis=0, tiled=True)  9.61 us
    all_to_all x2, starting transfers between devices, move_rows(): return lax.all_to_all(rows, 'band', split_axis=0, concat_axis=0, tiled=True)  8.9 us
    dot_general x4, matrix products, block_terms(): jnp.einsum('lu,xuh->xlh', normalized_cells, query_key_value_weight, prefe...  7.64 us
    dot_general x4, matrix products, block_terms(): jnp.einsum('bqhe,bkhe->bhqk', shaped[0], shaped[1], preferred_element_typ...  7.15 us
  transfers between devices with their start and end apart: 20, of which 19 were waited for; matrix products, arithmetic and copies ran while one was open for 17% of the time, Pallas kernels for 0%

profile of v1, /device:TPU:0, one launch (start us, length us, event | category | flops | bytes accessed | tf_op | source)
XLA Modules:
  0.0 236.2 jit_solution(8019089373825200144)
XLA Ops:
  7.7 4.8 %collective-permute-done = bf16[256,256]{1,0:T(8,128)(2,1)S(1)} collective-permute-done((bf16[256,256]{1,0:T(8,128)(2,1)}, bf16[256,256]{1,0:T(8,128)(2,1)S(1)}, u32[]{:S(2)}, u32[]{:S(2)}) %collective-permute-start) | collective-permute-done | bytes 131104 | tf_op jit(solution)/shard_map/ppermute | solution.py:24
  12.6 1.5 broadcast_compare_fusion
  14.1 2.9 %collective-permute-done.1 = bf16[256,256]{1,0:T(8,128)(2,1)S(1)} collective-permute-done((bf16[256,256]{1,0:T(8,128)(2,1)S(1)}, bf16[256,256]{1,0:T(8,128)(2,1)S(1)}, u32[]{:S(2)}, u32[]{:S(2)}) %collective-permute-start.1) | collective-permute-done | bytes 131104 | tf_op jit(solution)/shard_map/ppermute | solution.py:24
  17.0 4.4 %collective-permute-done.2 = bf16[256,256]{1,0:T(8,128)(2,1)S(1)} collective-permute-done((bf16[256,256]{1,0:T(8,128)(2,1)S(1)}, bf16[256,256]{1,0:T(8,128)(2,1)S(1)}, u32[]{:S(2)}, u32[]{:S(2)}) %collective-permute-start.2) | collective-permute-done | bytes 131104 | tf_op jit(solution)/shard_map/ppermute | solution.py:24
  26.6 1.1 reshape.424
  28.9 2.2 fusion.71
  31.7 1.2 fusion.26
  33.1 1.1 convolution_convert_fusion.3
  35.2 2.2 scatter_custom_fusion.1
  38.1 6.6 %all-to-all-start.1 = ((bf16[8,48,1]{1,2,0:T(2,128)(2,1)}), bf16[8,48,1]{1,2,0:T(2,128)(2,1)S(1)}, u32[]{:S(2)}, u32[]{:S(2)}) async-start(bf16[8,48,1]{1,2,0:T(2,128)(2,1)} %all_to_all.52), calls=%async_computation.2 | async-start | bytes 8192 | tf_op jit(solution)/shard_map/all_to_all | solution.py:118
  44.7 2.5 %scatter_custom_fusion.2 = bf16[384,256]{1,0:T(8,128)(2,1)} fusion(s32[256]{0:T(256)S(1)} %bitcast.215, bf16[256,256]{1,0:T(8,128)(2,1)} %param.21, bf16[]{:T(256)} %constant.27.clone.1), kind=kCustom, calls=%fused_computation.105 | custom fusion | bytes 197120 | tf_op jit(solution)/shard_map/scatter | solution.py:113
  47.2 4.0 %all-to-all-done.1 = bf16[8,48,1]{1,2,0:T(2,128)(2,1)S(1)} async-done(((bf16[8,48,1]{1,2,0:T(2,128)(2,1)}), bf16[8,48,1]{1,2,0:T(2,128)(2,1)S(1)}, u32[]{:S(2)}, u32[]{:S(2)}) %all-to-all-start.1) | async-done | bytes 800 | tf_op jit(solution)/shard_map/all_to_all | solution.py:118
  51.2 3.4 %all-to-all-start.3 = ((bf16[8,48,256]{2,1,0:T(8,128)(2,1)}), bf16[8,48,256]{2,1,0:T(8,128)(2,1)S(1)}, u32[]{:S(2)}, u32[]{:S(2)}) async-start(bf16[8,48,256]{2,1,0:T(8,128)(2,1)} %bitcast.34), calls=%async_computation.5 | async-start | bytes 393216 | tf_op jit(solution)/shard_map/all_to_all | solution.py:76
  54.6 3.5 %reduce-scatter.5.cloned.1.call-done = bf16[256,256]{1,0:T(8,128)(2,1)} async-done(((bf16[256,1024]{1,0:T(8,128)(2,1)}), bf16[256,256]{1,0:T(8,128)(2,1)}) %reduce-scatter.5.cloned.1.call-update) | async-done | bytes 131088 | tf_op jit(solution)/shard_map/reduce_scatter | solution.py:70
  58.1 2.5 %scatter_custom_fusion = bf16[384,256]{1,0:T(8,128)(2,1)} fusion(s32[256]{0:T(256)S(1)} %bitcast.216, bf16[256,256]{1,0:T(8,128)(2,1)} %reduce-scatter.5.cloned.1.call-done, bf16[256,256]{1,0:T(8,128)(2,1)S(1)} %copy-done.15, bf16[]{:T(256)} %constant.27.clone.1), kind=kCustom, calls=%fused_computation.100 | custom fusion | flops 262144 | bytes 458754 | tf_op jit(solution)/shard_map/scatter | solution.py:115
  60.6 1.7 all-to-all-done.3
  62.3 3.8 %all-to-all-start = ((bf16[8,48,256]{2,1,0:T(8,128)(2,1)}), bf16[8,48,256]{2,1,0:T(8,128)(2,1)S(1)}, u32[]{:S(2)}, u32[]{:S(2)}) async-start(bf16[8,48,256]{2,1,0:T(8,128)(2,1)} %bitcast.16), calls=%async_computation.1 | async-start | bytes 393216 | tf_op jit(solution)/shard_map/all_to_all | solution.py:117
  66.3 5.0 %collective-permute-done.6 = bf16[384,256]{1,0:T(8,128)(2,1)S(1)} collective-permute-done((bf16[384,256]{1,0:T(8,128)(2,1)S(1)}, bf16[384,256]{1,0:T(8,128)(2,1)S(1)}, u32[]{:S(2)}, u32[]{:S(2)}) %collective-permute-start.6) | collective-permute-done | bytes 196640 | tf_op jit(solution)/shard_map/ppermute | solution.py:24
  71.3 2.7 %all-to-all-done = bf16[8,48,256]{2,1,0:T(8,128)(2,1)S(1)} async-done(((bf16[8,48,256]{2,1,0:T(8,128)(2,1)}), bf16[8,48,256]{2,1,0:T(8,128)(2,1)S(1)}, u32[]{:S(2)}, u32[]{:S(2)}) %all-to-all-start) | async-done | bytes 196640 | tf_op jit(solution)/shard_map/all_to_all | solution.py:117
  74.1 2.3 collective-permute-done.7
  76.4 2.9 %collective-permute-done.3 = bf16[384,256]{1,0:T(8,128)(2,1)} collective-permute-done((bf16[384,256]{1,0:T(8,128)(2,1)S(1)}, bf16[384,256]{1,0:T(8,128)(2,1)}, u32[]{:S(2)}, u32[]{:S(2)}) %collective-permute-start.3) | collective-permute-done | bytes 196640 | tf_op jit(solution)/shard_map/ppermute | solution.py:24
  80.2 1.3 collective-permute-done.8
  81.5 1.2 pad_maximum_fusion.1
  82.7 1.6 gather_fusion.3
  84.4 1.5 copy.77
  86.1 2.2 convolution_convert_fusion.6
  88.3 3.1 %collective-permute-done.5 = bf16[384,256]{1,0:T(8,128)(2,1)S(1)} collective-permute-done((bf16[384,256]{1,0:T(8,128)(2,1)}, bf16[384,256]{1,0:T(8,128)(2,1)S(1)}, u32[]{:S(2)}, u32[]{:S(2)}) %collective-permute-start.5) | collective-permute-done | bytes 196640 | tf_op jit(solution)/shard_map/ppermute | solution.py:24
  91.4 2.1 pad_maximum_fusion
  93.5 1.9 gather_fusion.1
  95.4 1.3 convert_bitcast_fusion
  97.5 3.0 %copy.72 = f32[384,4,256]{0,2,1:T(8,128)} copy(f32[384,4,256]{2,0,1:T(8,128)} %convert_bitcast_fusion) | data formatting | bytes 3145728 | tf_op jit(solution)/shard_map/jvp()/convert_element_type | solution.py:35
  100.5 3.0 %copy.73 = f32[384,1024]{1,0:T(8,128)} copy(f32[384,1024]{0,1:T(8,128)} %bitcast.176) | data formatting | bytes 3145728 | tf_op jit(solution)/shard_map/jvp()/convert_element_type | solution.py:35
  104.1 2.5 %fusion.15 = bf16[3,384,256]{1,2,0:T(8,128)(2,1)S(1)} fusion(bf16[3,1024,256]{2,1,0:T(8,128)(2,1)S(1)} %copy-done, f32[384,1024]{1,0:T(8,128)} %copy.73, f32[1024]{0:T(1024)S(1)} %copy-done.24, f32[384]{0:T(512)S(1)} %fusion.56), kind=kOutput, calls=%fused_computation.44 | convolution fusion | flops 605454336 | bytes 3741184 | tf_op jit(solution)/shard_map/jvp(lu,xuh->xlh)/dot_general | solution.py:38
  106.7 2.9 %fusion.72 = (f32[4,384]{1,0:T(4,128)}, f32[4,384,384]{1,2,0:T(8,128)}) fusion(pred[384,384]{0,1:T(8,128)(4,1)S(1)} %fusion.37, bf16[384,4,64]{0,2,1:T(8,128)(2,1)S(1)} %bitcast.202, bf16[384,4,64]{0,2,1:T(8,128)(2,1)S(1)} %bitcast.199), kind=kOutput, calls=%fused_computation.144 | convolution fusion | flops 77857152 | bytes 2906112 | tf_op jit(solution)/shard_map/jvp()/sub | solution.py:49
  110.4 3.7 %fusion.7 = (f32[4,384]{1,0:T(4,128)S(1)}, bf16[4,384,384]{1,2,0:T(8,128)(2,1)}, bf16[4,384,384]{1,2,0:T(8,128)(2,1)}) fusion(f32[4,384,384]{1,2,0:T(8,128)} %get-tuple-element.13, f32[4,384]{1,0:T(4,128)S(1)} %multiply_divide_fusion, f32[4,384]{1,0:T(4,128)} %get-tuple-element.12, bf16[4,64,384]{2,1,0:T(8,128)(2,1)S(1)} %bitcast.190, ...), kind=kOutput, calls=%fused_computation.19 | convolution fusion | flops 79624704 | bytes 5130240 | tf_op jit(solution)/shard_map/transpose(jvp(bhqk,bkhe->bqhe))/dot_general | solution.py:52
  114.7 3.0 %fusion.23 = bf16[1,1,384,4,64]{2,4,3,1,0:T(8,128)(2,1)S(1)} fusion(bf16[384,4,64]{0,2,1:T(8,128)(2,1)S(1)} %bitcast.203, bf16[4,384,384]{1,2,0:T(8,128)(2,1)} %get-tuple-element.14, f32[4,384]{1,0:T(4,128)} %neg.13, f32[4,384]{1,0:T(4,128)} %get-tuple-element.12, pred[384,384]{0,1:T(8,128)(4,1)S(1)} %fusion.37, bf16[384,4,64]{0,2,1:T(8,128)(2,1)S(1)} %bitcast.200), kind=kOutput, calls=%fused_computation.60 | convolution fusion | flops 156403584 | bytes 1929216 | tf_op jit(solution)/shard_map/transpose(jvp(bqhe,bkhe->bhqk))/dot_general | solution.py:45
  117.7 3.6 %fusion.24 = bf16[1,1,384,4,64]{2,4,3,1,0:T(8,128)(2,1)} fusion(bf16[384,4,64]{0,2,1:T(8,128)(2,1)S(1)} %bitcast.201, bf16[4,384,384]{1,2,0:T(8,128)(2,1)} %get-tuple-element.14, f32[4,384]{1,0:T(4,128)} %neg.13, f32[4,384]{1,0:T(4,128)} %get-tuple-element.12, pred[384,384]{0,1:T(8,128)(4,1)S(1)} %fusion.37, bf16[384,4,64]{0,2,1:T(8,128)(2,1)S(1)} %bitcast.204), kind=kOutput, calls=%fused_computation.61 | convolution fusion | flops 156403584 | bytes 1929216 | tf_op jit(solution)/shard_map/transpose(jvp(bqhe,bkhe->bhqk))/dot_general | solution.py:45
  121.3 1.8 fusion.25
  123.1 1.8 pad_add_fusion
  124.9 1.3 copy.81
  126.3 2.4 %multiply_reduce_fusion = (f32[384]{0:T(512)S(1)}, bf16[384,1024]{1,0:T(8,128)(2,1)S(1)}) fusion(f32[384,1024]{1,0:T(8,128)} %copy.73, f32[1024]{0:T(1024)S(1)} %copy-done.25, bf16[3,1024,256]{2,1,0:T(8,128)(2,1)S(1)} %copy-done, bf16[3,384,256]{2,1,0:T(8,128)(2,1)S(1)} %copy.81), kind=kOutput, calls=%fused_computation.30 | convolution fusion | flops 605945472 | bytes 4527616 | tf_op jit(solution)/shard_map/transpose(jvp(lu,xuh->xlh))/dot_general | solution.py:38
  128.8 1.3 fusion.10
  130.1 24.3 %reduce-scatter.9.cloned.1.call-done = bf16[384,256]{1,0:T(8,128)(2,1)} async-done(((bf16[384,1024]{1,0:T(8,128)(2,1)}), bf16[384,256]{1,0:T(8,128)(2,1)}) %reduce-scatter.9.cloned.1.call-update) | async-done | bytes 196624 | tf_op jit(solution)/shard_map/reduce_scatter | solution.py:70
  154.4 1.7 add_convert_fusion
  156.0 5.5 %all-to-all-start.4 = ((bf16[8,48,256]{2,1,0:T(8,128)(2,1)}), bf16[8,48,256]{2,1,0:T(8,128)(2,1)S(1)}, u32[]{:S(2)}, u32[]{:S(2)}) async-start(bf16[8,48,256]{2,1,0:T(8,128)(2,1)} %bitcast.59), calls=%async_computation.7 | async-start | bytes 393216 | tf_op jit(solution)/shard_map/all_to_all | solution.py:76
  161.6 7.9 %all-to-all-done.4 = bf16[8,48,256]{2,1,0:T(8,128)(2,1)S(1)} async-done(((bf16[8,48,256]{2,1,0:T(8,128)(2,1)}), bf16[8,48,256]{2,1,0:T(8,128)(2,1)S(1)}, u32[]{:S(2)}, u32[]{:S(2)}) %all-to-all-start.4) | async-done | bytes 196640 | tf_op jit(solution)/shard_map/all_to_all | solution.py:76
  169.5 1.2 gather_fusion.4
  170.7 4.4 %collective-permute-done.9 = bf16[256,256]{1,0:T(8,128)(2,1)S(1)} collective-permute-done((bf16[256,256]{1,0:T(8,128)(2,1)S(1)}, bf16[256,256]{1,0:T(8,128)(2,1)S(1)}, u32[]{:S(2)}, u32[]{:S(2)}) %collective-permute-start.9) | collective-permute-done | bytes 131104 | tf_op jit(solution)/shard_map/ppermute | solution.py:24
  175.7 1.7 convolution_convert_fusion.10
  177.4 2.8 %collective-permute-done.10 = bf16[256,256]{1,0:T(8,128)(2,1)} collective-permute-done((bf16[256,256]{1,0:T(8,128)(2,1)S(1)}, bf16[256,256]{1,0:T(8,128)(2,1)}, u32[]{:S(2)}, u32[]{:S(2)}) %collective-permute-start.10) | collective-permute-done | bytes 131104 | tf_op jit(solution)/shard_map/ppermute | solution.py:24
  180.2 1.3 convolution_convert_fusion.1
  181.8 3.1 %collective-permute-done.11 = bf16[256,256]{1,0:T(8,128)(2,1)} collective-permute-done((bf16[256,256]{1,0:T(8,128)(2,1)}, bf16[256,256]{1,0:T(8,128)(2,1)}, u32[]{:S(2)}, u32[]{:S(2)}) %collective-permute-start.11) | collective-permute-done | bytes 131104 | tf_op jit(solution)/shard_map/ppermute | solution.py:24
  185.0 2.0 pad_maximum_fusion.3
  187.0 2.6 %gather_fusion.5 = bf16[4,256,256]{2,1,0:T(8,128)(2,1)} fusion(bf16[4,256,256]{2,1,0:T(8,128)(2,1)} %pad_maximum_fusion.3, s32[1024]{0:T(1024)} %copy-done.33), kind=kCustom, calls=%fused_computation.5 | custom fusion | bytes 1048592 | tf_op jit(solution)/shard_map/gather | solution.py:27
  189.6 2.1 copy.84
  191.6 1.4 convolution_convert_fusion.14
  194.8 1.4 multiply_reduce_fusion.2
  196.2 1.4 fusion.27
  198.9 2.1 multiply_reduce_fusion.1
  202.1 1.7 reduce-scatter.7.cloned.1.call-done
  204.8 13.3 %all_to_all.58 = bf16[8,48,256]{2,1,0:T(8,128)(2,1)S(1)} all-to-all(bf16[8,48,256]{2,1,0:T(8,128)(2,1)S(1)} %bitcast.189), channel_id=1, replica_groups=mesh['band'=8,'mp'=4] {'band'}, dimensions={0} | all-to-all | bytes 393216 | tf_op jit(solution)/shard_map/all_to_all | solution.py:76
  218.1 1.8 gather_fusion.2
  219.9 8.1 %reduce-scatter.11.cloned.1.call-done = bf16[256,256]{1,0:T(8,128)(2,1)} async-done(((bf16[256,1024]{1,0:T(8,128)(2,1)}), bf16[256,256]{1,0:T(8,128)(2,1)}) %reduce-scatter.11.cloned.1.call-update) | async-done | bytes 131088 | tf_op jit(solution)/shard_map/reduce_scatter | solution.py:70
  228.0 1.6 add_convert_fusion.2
  (153 shorter events, 19.7 us)
Async XLA Ops:
  7.2 97.0 %copy-start = (bf16[3,1024,256]{2,1,0:T(8,128)(2,1)S(1)}, bf16[3,1024,256]{2,1,0:T(8,128)(2,1)}, u32[]{:S(2)}) copy-start(bf16[3,1024,256]{2,1,0:T(8,128)(2,1)} %param.16) | copy-start | bytes 4718596
  7.2 50.9 %reduce-scatter.5.cloned.1.call-start = ((), (), s32[]{:S(2)}) async-start(), calls=%async_computation.9 | async-start | bytes 655360 | tf_op jit(solution)/shard_map/reduce_scatter | solution.py:70
  7.2 5.3 %collective-permute-start = (bf16[256,256]{1,0:T(8,128)(2,1)}, bf16[256,256]{1,0:T(8,128)(2,1)S(1)}, u32[]{:S(2)}, u32[]{:S(2)}) collective-permute-start(bf16[256,256]{1,0:T(8,128)(2,1)} %param.11), channel_id=1, source_target_pairs={{0,1},{1,2},{2,3},{3,0},{4,5},{5,6},{6,7},{7,4},{8,9},{9,10},{10,1... | collective-permute-start | bytes 393224 | tf_op jit(solution)/shard_map/ppermute | solution.py:24
  12.5 4.4 %collective-permute-start.1 = (bf16[256,256]{1,0:T(8,128)(2,1)S(1)}, bf16[256,256]{1,0:T(8,128)(2,1)S(1)}, u32[]{:S(2)}, u32[]{:S(2)}) collective-permute-start(bf16[256,256]{1,0:T(8,128)(2,1)S(1)} %collective-permute-done), channel_id=1, source_target_pairs={{0,1},{1,2},{2,3},{3,0},{4,5},{5,6},{6,7},{7,4},{8,9},{9,10},{10,1... | collective-permute-start | bytes 393224 | tf_op jit(solution)/shard_map/ppermute | solution.py:24
  16.9 4.4 %collective-permute-start.2 = (bf16[256,256]{1,0:T(8,128)(2,1)S(1)}, bf16[256,256]{1,0:T(8,128)(2,1)S(1)}, u32[]{:S(2)}, u32[]{:S(2)}) collective-permute-start(bf16[256,256]{1,0:T(8,128)(2,1)S(1)} %collective-permute-done.1), channel_id=1, source_target_pairs={{0,1},{1,2},{2,3},{3,0},{4,5},{5,6},{6,7},{7,4},{8,9},{9,10},{10,1... | collective-permute-start | bytes 393224 | tf_op jit(solution)/shard_map/ppermute | solution.py:24
  16.9 6.4 %copy-start.33 = (s32[1024]{0:T(1024)}, s32[1024]{0:T(1024)S(1)}, u32[]{:S(2)}) copy-start(s32[1024]{0:T(1024)S(1)} %pad_clamp_fusion.1) | copy-start | bytes 12292
  22.9 1.4 copy-start.2
  22.9 1.4 copy-start.26
  23.2 0.6 copy-start.31
  23.7 1.9 copy-start.29
  26.6 6.5 %copy-start.4 = (bf16[256,1024]{1,0:T(8,128)(2,1)S(1)}, bf16[256,1024]{1,0:T(8,128)(2,1)}, u32[]{:S(2)}) copy-start(bf16[256,1024]{1,0:T(8,128)(2,1)} %param.14) | copy-start | bytes 1572868
  28.9 5.4 %copy-start.12 = (bf16[2,128,4,64]{1,3,2,0:T(8,128)(2,1)}, bf16[2,128,4,64]{1,3,2,0:T(8,128)(2,1)S(1)}, u32[]{:S(2)}) copy-start(bf16[2,128,4,64]{1,3,2,0:T(8,128)(2,1)S(1)} %copy.69) | copy-start | bytes 393220
  28.9 5.4 %copy-start.34 = (s32[256,1]{0,1:T(1,128)S(1)}, s32[256,1]{0,1:T(1,128)}, u32[]{:S(2)}) copy-start(s32[256,1]{0,1:T(1,128)} %param.19) | copy-start | bytes 3076
  28.9 6.2 %copy-start.41 = (s32[256]{0:T(256)S(1)}, s32[256]{0:T(256)}, u32[]{:S(2)}) copy-start(s32[256]{0:T(256)} %param.20) | copy-start | bytes 3076
  31.1 0.6 copy-start.39
  31.1 27.0 %copy-start.15 = (bf16[256,256]{1,0:T(8,128)(2,1)S(1)}, bf16[256,256]{1,0:T(8,128)(2,1)}, u32[]{:S(2)}) copy-start(bf16[256,256]{1,0:T(8,128)(2,1)} %param.11) | copy-start | bytes 393220
  35.2 30.9 %copy-start.37 = (s32[256,1]{0,1:T(1,128)}, s32[256,1]{0,1:T(1,128)S(1)}, u32[]{:S(2)}) copy-start(s32[256,1]{0,1:T(1,128)S(1)} %compare_select_fusion) | copy-start | bytes 3076
  38.1 13.1 %all-to-all-start.1 = ((bf16[8,48,1]{1,2,0:T(2,128)(2,1)}), bf16[8,48,1]{1,2,0:T(2,128)(2,1)S(1)}, u32[]{:S(2)}, u32[]{:S(2)}) async-start(bf16[8,48,1]{1,2,0:T(2,128)(2,1)} %all_to_all.52), calls=%async_computation.2 | async-start | bytes 8192 | tf_op jit(solution)/shard_map/all_to_all | solution.py:118
  51.2 11.1 %all-to-all-start.3 = ((bf16[8,48,256]{2,1,0:T(8,128)(2,1)}), bf16[8,48,256]{2,1,0:T(8,128)(2,1)S(1)}, u32[]{:S(2)}, u32[]{:S(2)}) async-start(bf16[8,48,256]{2,1,0:T(8,128)(2,1)} %bitcast.34), calls=%async_computation.5 | async-start | bytes 393216 | tf_op jit(solution)/shard_map/all_to_all | solution.py:76
  62.3 19.2 %copy-start.8 = (bf16[8,48,256]{2,1,0:T(8,128)(2,1)}, bf16[8,48,256]{2,1,0:T(8,128)(2,1)S(1)}, u32[]{:S(2)}) copy-start(bf16[8,48,256]{2,1,0:T(8,128)(2,1)S(1)} %all-to-all-done.3) | copy-start | bytes 589828
  62.3 11.8 %all-to-all-start = ((bf16[8,48,256]{2,1,0:T(8,128)(2,1)}), bf16[8,48,256]{2,1,0:T(8,128)(2,1)S(1)}, u32[]{:S(2)}, u32[]{:S(2)}) async-start(bf16[8,48,256]{2,1,0:T(8,128)(2,1)} %bitcast.16), calls=%async_computation.1 | async-start | bytes 393216 | tf_op jit(solution)/shard_map/all_to_all | solution.py:117
  66.1 88.3 %reduce-scatter.9.cloned.1.call-start = ((), (), s32[]{:S(2)}) async-start(), calls=%async_computation.11 | async-start | bytes 983040 | tf_op jit(solution)/shard_map/reduce_scatter | solution.py:70
  66.2 5.1 %collective-permute-start.6 = (bf16[384,256]{1,0:T(8,128)(2,1)S(1)}, bf16[384,256]{1,0:T(8,128)(2,1)S(1)}, u32[]{:S(2)}, u32[]{:S(2)}) collective-permute-start(bf16[384,256]{1,0:T(8,128)(2,1)S(1)} %bitcast.184), channel_id=1, source_target_pairs={{0,1},{1,2},{2,3},{3,0},{4,5},{5,6},{6,7},{7,4},{8,9},{9,10},{10,1... | collective-permute-start | bytes 589832 | tf_op jit(solution)/shard_map/ppermute | solution.py:24
  66.3 12.9 %copy-start.28 = (bf16[384]{0:T(512)(128)(2,1)}, bf16[384]{0:T(512)(128)(2,1)S(1)}, u32[]{:S(2)}) copy-start(bf16[384]{0:T(512)(128)(2,1)S(1)} %eq.97) | copy-start | bytes 2308
  71.3 10.2 %copy-start.16 = (bf16[384,256]{1,0:T(8,128)(2,1)}, bf16[384,256]{1,0:T(8,128)(2,1)S(1)}, u32[]{:S(2)}) copy-start(bf16[384,256]{1,0:T(8,128)(2,1)S(1)} %collective-permute-done.6) | copy-start | bytes 589828
  71.3 5.1 %collective-permute-start.7 = (bf16[384,256]{1,0:T(8,128)(2,1)S(1)}, bf16[384,256]{1,0:T(8,128)(2,1)S(1)}, u32[]{:S(2)}, u32[]{:S(2)}) collective-permute-start(bf16[384,256]{1,0:T(8,128)(2,1)S(1)} %collective-permute-done.6), channel_id=1, source_target_pairs={{0,1},{1,2},{2,3},{3,0},{4,5},{5,6},{6,7},{7,4},{8,9},{9,10},{10,1... | collective-permute-start | bytes 589832 | tf_op jit(solution)/shard_map/ppermute | solution.py:24
  74.1 7.5 %copy-start.6 = (bf16[8,48,256]{2,1,0:T(8,128)(2,1)}, bf16[8,48,256]{2,1,0:T(8,128)(2,1)S(1)}, u32[]{:S(2)}) copy-start(bf16[8,48,256]{2,1,0:T(8,128)(2,1)S(1)} %all-to-all-done) | copy-start | bytes 589828
  74.1 5.2 %collective-permute-start.3 = (bf16[384,256]{1,0:T(8,128)(2,1)S(1)}, bf16[384,256]{1,0:T(8,128)(2,1)}, u32[]{:S(2)}, u32[]{:S(2)}) collective-permute-start(bf16[384,256]{1,0:T(8,128)(2,1)S(1)} %bitcast.182), channel_id=1, source_target_pairs={{0,1},{1,2},{2,3},{3,0},{4,5},{5,6},{6,7},{7,4},{8,9},{9,10},{10,1... | collective-permute-start | bytes 589832 | tf_op jit(solution)/shard_map/ppermute | solution.py:24
  76.4 5.1 %copy-start.17 = (bf16[384,256]{1,0:T(8,128)(2,1)}, bf16[384,256]{1,0:T(8,128)(2,1)S(1)}, u32[]{:S(2)}) copy-start(bf16[384,256]{1,0:T(8,128)(2,1)S(1)} %collective-permute-done.7) | copy-start | bytes 589828
  76.4 5.1 %collective-permute-start.8 = (bf16[384,256]{1,0:T(8,128)(2,1)S(1)}, bf16[384,256]{1,0:T(8,128)(2,1)S(1)}, u32[]{:S(2)}, u32[]{:S(2)}) collective-permute-start(bf16[384,256]{1,0:T(8,128)(2,1)S(1)} %collective-permute-done.7), channel_id=1, source_target_pairs={{0,1},{1,2},{2,3},{3,0},{4,5},{5,6},{6,7},{7,4},{8,9},{9,10},{10,1... | collective-permute-start | bytes 589832 | tf_op jit(solution)/shard_map/ppermute | solution.py:24
  79.3 6.6 %collective-permute-start.4 = (bf16[384,256]{1,0:T(8,128)(2,1)}, bf16[384,256]{1,0:T(8,128)(2,1)}, u32[]{:S(2)}, u32[]{:S(2)}) collective-permute-start(bf16[384,256]{1,0:T(8,128)(2,1)} %collective-permute-done.3), channel_id=1, source_target_pairs={{0,1},{1,2},{2,3},{3,0},{4,5},{5,6},{6,7},{7,4},{8,9},{9,10},{10,1... | collective-permute-start | bytes 589832 | tf_op jit(solution)/shard_map/ppermute | solution.py:24
  85.9 5.5 %collective-permute-start.5 = (bf16[384,256]{1,0:T(8,128)(2,1)}, bf16[384,256]{1,0:T(8,128)(2,1)S(1)}, u32[]{:S(2)}, u32[]{:S(2)}) collective-permute-start(bf16[384,256]{1,0:T(8,128)(2,1)} %collective-permute-done.4), channel_id=1, source_target_pairs={{0,1},{1,2},{2,3},{3,0},{4,5},{5,6},{6,7},{7,4},{8,9},{9,10},{10,1... | collective-permute-start | bytes 589832 | tf_op jit(solution)/shard_map/ppermute | solution.py:24
  100.5 3.0 %copy-start.22 = (f32[384]{0:T(512)S(1)}, f32[384]{0:T(512)}, u32[]{:S(2)}) copy-start(f32[384]{0:T(512)} %fusion.9) | copy-start | bytes 4612
  100.5 3.6 %copy-start.24 = (f32[1024]{0:T(1024)S(1)}, f32[1024]{0:T(1024)}, u32[]{:S(2)}) copy-start(f32[1024]{0:T(1024)} %param.15) | copy-start | bytes 12292
  103.6 0.6 copy-start.35
  106.7 7.4 %copy-start.10 = (bf16[1,384,256]{1,2,0:T(8,128)(2,1)}, bf16[1,384,256]{1,2,0:T(8,128)(2,1)S(1)}, u32[]{:S(2)}) copy-start(bf16[1,384,256]{1,2,0:T(8,128)(2,1)S(1)} %get-tuple-element.6) | copy-start | bytes 589828
  106.7 3.7 %copy-start.11 = (bf16[384,256]{0,1:T(8,128)(2,1)S(1)}, bf16[384,256]{0,1:T(8,128)(2,1)}, u32[]{:S(2)}) copy-start(bf16[384,256]{0,1:T(8,128)(2,1)} %convolution_convert_fusion.6) | copy-start | bytes 589828
  121.3 4.9 %copy-start.25 = (f32[1024]{0:T(1024)S(1)}, f32[1024]{0:T(1024)}, u32[]{:S(2)}) copy-start(f32[1024]{0:T(1024)} %param.15) | copy-start | bytes 12292
  126.2 2.5 %copy-start.23 = (f32[384]{0:T(512)S(1)}, f32[384]{0:T(512)}, u32[]{:S(2)}) copy-start(f32[384]{0:T(512)} %fusion.9) | copy-start | bytes 4612
  126.3 2.5 %copy-start.1 = (f32[384,1024]{1,0:T(8,128)S(1)}, f32[384,1024]{1,0:T(8,128)}, u32[]{:S(2)}) copy-start(f32[384,1024]{1,0:T(8,128)} %copy.73) | copy-start | bytes 4718596
  126.3 2.5 %copy-start.36 = (f32[384]{0:T(512)S(1)}, f32[384]{0:T(512)}, u32[]{:S(2)}) copy-start(f32[384]{0:T(512)} %copy-done.35) | copy-start | bytes 4612
  128.7 25.7 %copy-start.9 = (bf16[8,48,256]{2,1,0:T(8,128)(2,1)S(1)}, bf16[8,48,256]{2,1,0:T(8,128)(2,1)}, u32[]{:S(2)}) copy-start(bf16[8,48,256]{2,1,0:T(8,128)(2,1)} %copy-done.8) | copy-start | bytes 589828
  128.7 32.9 %copy-start.38 = (s32[256,1]{0,1:T(1,128)S(1)}, s32[256,1]{0,1:T(1,128)}, u32[]{:S(2)}) copy-start(s32[256,1]{0,1:T(1,128)} %copy-done.37) | copy-start | bytes 3076
  128.7 42.0 %copy-start.40 = (f32[2,4,128]{2,1,0:T(4,128)S(1)}, f32[2,4,128]{2,1,0:T(4,128)}, u32[]{:S(2)}) copy-start(f32[2,4,128]{2,1,0:T(4,128)} %copy-done.39) | copy-start | bytes 12292
  130.0 50.2 %copy-start.3 = (bf16[256,1024]{1,0:T(8,128)(2,1)S(1)}, bf16[256,1024]{1,0:T(8,128)(2,1)}, u32[]{:S(2)}) copy-start(bf16[256,1024]{1,0:T(8,128)(2,1)} %param.17) | copy-start | bytes 1572868
  156.0 13.5 %all-to-all-start.4 = ((bf16[8,48,256]{2,1,0:T(8,128)(2,1)}), bf16[8,48,256]{2,1,0:T(8,128)(2,1)S(1)}, u32[]{:S(2)}, u32[]{:S(2)}) async-start(bf16[8,48,256]{2,1,0:T(8,128)(2,1)} %bitcast.59), calls=%async_computation.7 | async-start | bytes 393216 | tf_op jit(solution)/shard_map/all_to_all | solution.py:76
  161.5 42.3 %reduce-scatter.7.cloned.1.call-start = ((), (), s32[]{:S(2)}) async-start(), calls=%async_computation.10 | async-start | bytes 983040 | tf_op jit(solution)/shard_map/reduce_scatter | solution.py:70
  170.7 4.4 %collective-permute-start.9 = (bf16[256,256]{1,0:T(8,128)(2,1)S(1)}, bf16[256,256]{1,0:T(8,128)(2,1)S(1)}, u32[]{:S(2)}, u32[]{:S(2)}) collective-permute-start(bf16[256,256]{1,0:T(8,128)(2,1)S(1)} %gather_fusion.4), channel_id=1, source_target_pairs={{0,1},{1,2},{2,3},{3,0},{4,5},{5,6},{6,7},{7,4},{8,9},{9,10},{10,1... | collective-permute-start | bytes 393224 | tf_op jit(solution)/shard_map/ppermute | solution.py:24
  175.1 0.6 copy-start.20
  175.7 4.5 %collective-permute-start.10 = (bf16[256,256]{1,0:T(8,128)(2,1)S(1)}, bf16[256,256]{1,0:T(8,128)(2,1)}, u32[]{:S(2)}, u32[]{:S(2)}) collective-permute-start(bf16[256,256]{1,0:T(8,128)(2,1)S(1)} %collective-permute-done.9), channel_id=1, source_target_pairs={{0,1},{1,2},{2,3},{3,0},{4,5},{5,6},{6,7},{7,4},{8,9},{9,10},{10,1... | collective-permute-start | bytes 393224 | tf_op jit(solution)/shard_map/ppermute | solution.py:24
  180.2 4.7 %collective-permute-start.11 = (bf16[256,256]{1,0:T(8,128)(2,1)}, bf16[256,256]{1,0:T(8,128)(2,1)}, u32[]{:S(2)}, u32[]{:S(2)}) collective-permute-start(bf16[256,256]{1,0:T(8,128)(2,1)} %collective-permute-done.10), channel_id=1, source_target_pairs={{0,1},{1,2},{2,3},{3,0},{4,5},{5,6},{6,7},{7,4},{8,9},{9,10},{10,1... | collective-permute-start | bytes 393224 | tf_op jit(solution)/shard_map/ppermute | solution.py:24
  181.5 10.1 %copy-start.5 = (bf16[256,1024]{1,0:T(8,128)(2,1)S(1)}, bf16[256,1024]{1,0:T(8,128)(2,1)}, u32[]{:S(2)}) copy-start(bf16[256,1024]{1,0:T(8,128)(2,1)} %param.14) | copy-start | bytes 1572868
  181.6 46.5 %reduce-scatter.11.cloned.1.call-start = ((), (), s32[]{:S(2)}) async-start(), calls=%async_computation.12 | async-start | bytes 655360 | tf_op jit(solution)/shard_map/reduce_scatter | solution.py:70
  185.0 9.8 %copy-start.13 = (bf16[2,128,4,64]{1,3,2,0:T(8,128)(2,1)S(1)}, bf16[2,128,4,64]{1,3,2,0:T(8,128)(2,1)}, u32[]{:S(2)}) copy-start(bf16[2,128,4,64]{1,3,2,0:T(8,128)(2,1)} %copy-done.12) | copy-start | bytes 393220
  193.0 4.5 %copy-start.14 = (f32[2,4,128,128]{2,3,1,0:T(8,128)S(1)}, f32[2,4,128,128]{2,3,1,0:T(8,128)}, u32[]{:S(2)}) copy-start(f32[2,4,128,128]{2,3,1,0:T(8,128)} %get-tuple-element.11) | copy-start | bytes 1572868
  194.7 2.8 %copy-start.19 = (bf16[2,128,4,64]{1,3,2,0:T(8,128)(2,1)S(1)}, bf16[2,128,4,64]{1,3,2,0:T(8,128)(2,1)}, u32[]{:S(2)}) copy-start(bf16[2,128,4,64]{1,3,2,0:T(8,128)(2,1)} %copy.68) | copy-start | bytes 393220
  194.7 2.8 %copy-start.21 = (pred[2,128,128]{1,2,0:T(8,128)(4,1)S(1)}, pred[2,128,128]{1,2,0:T(8,128)(4,1)}, u32[]{:S(2)}) copy-start(pred[2,128,128]{1,2,0:T(8,128)(4,1)} %broadcast_compare_fusion) | copy-start | bytes 98308
  196.1 1.7 copy-start.18
  197.8 1.1 copy-start.27
  198.6 2.4 %copy-start.32 = (f32[256]{0:T(256)S(1)}, f32[256]{0:T(256)}, u32[]{:S(2)}) copy-start(f32[256]{0:T(256)} %copy-done.31) | copy-start | bytes 3076
  198.6 2.4 %copy-start.30 = (f32[256]{0:T(256)S(1)}, f32[256]{0:T(256)}, u32[]{:S(2)}) copy-start(f32[256]{0:T(256)} %copy-done.29) | copy-start | bytes 3076
  201.0 2.8 %copy-start.7 = (bf16[8,48,256]{2,1,0:T(8,128)(2,1)S(1)}, bf16[8,48,256]{2,1,0:T(8,128)(2,1)}, u32[]{:S(2)}) copy-start(bf16[8,48,256]{2,1,0:T(8,128)(2,1)} %copy-done.6) | copy-start | bytes 589828
Sparse Core Ops, SparseCore 0:
  34.3 23.7 reduce-scatter.4
  130.2 24.1 reduce-scatter.8
  181.7 22.1 reduce-scatter.6
  206.3 21.6 reduce-scatter.10
